TPU v7x, 1024 devices: a whole 4x8x16 slice. The times are simulated.
1024 devices in a mesh: dp: 16 (over y, core), rows: 64 (over z, x).
Axes of the slice: x: 4, y: 8, z: 16, core: 2. Of those that a mesh axis runs over, the one named last changes fastest.
Arguments:
- item_table: float32 [131072, 256], P('rows'), may hold values from -0.5 to 0.5
- row_accum: float32 [131072], P('rows'), may hold values from 0.1 to 10
- owner_map: int32 [16, 64, 512, 1], P('dp', 'rows'), may hold values from 0 to 63; in each aligned block of 512 rows (0 to 511, 512 to 1023, ..., all dimensions but the last counted through in order) at most 24 rows name the same one
- row_index: int32 [16, 64, 512], P('dp', 'rows'), may hold values from 0 to 2047
- bag_index: int32 [16, 64, 512], P('dp', 'rows'), may hold values from 0 to 3, never falling along the last dimension, each value on 1 to 256 neighbouring positions
- prev_owner: int32 [16, 64, 512, 1], P('dp', 'rows'), may hold values from 0 to 63; in each aligned block of 512 rows (0 to 511, 512 to 1023, ..., all dimensions but the last counted through in order) at most 24 rows name the same one
- prev_row: int32 [16, 64, 512], P('dp', 'rows'), may hold values from 0 to 2047
- prev_bag: int32 [16, 64, 512], P('dp', 'rows'), may hold values from 0 to 3, never falling along the last dimension, each value on 1 to 256 neighbouring positions
- grad_pooled: float32 [16, 64, 4, 256], P('dp', 'rows'), may hold values from -6 to 6
Outputs:
- pooled: float32 [16, 64, 4, 256], P('dp', 'rows')
- new_table: float32 [131072, 256], P('rows')
- new_accum: float32 [131072], P('rows')
Inputs may be any that keep to these rules, and one draw needn't show every extreme that they name: `owner_map`: among the positions of one device no owner is named more than 24 times, a bound that some block reaches. `prev_owner`: among the positions of one device no owner is named more than 24 times, a bound that some block reaches. `bag_index`: never falls along a device's positions; every bag has 1 to 256 positions, one exactly 256. `prev_bag`: never falls along a device's positions; every bag has 1 to 256 positions, one exactly 256.
All inputs are finite; a program needn't handle non-finite values.
Results may differ from a plain program's by a relative error of at most 0.0003.
Values sent between devices are 32-bit elements; how exact they have to be, the bound alone decides.
A program may use at most 32 MiB of HBM per device.

v0:
```python
import jax
import jax.numpy as jnp
from jax import lax
from jax.sharding import PartitionSpec as P

learn_rate = 0.1


def slot_numbers(owner_column, owners, capacity):
    owned = owner_column[:, 0]
    onehot = (owned[:, None] == jnp.arange(owners)[None, :]).astype(jnp.int32)
    placed = jnp.sum((jnp.cumsum(onehot, axis=0) - 1) * onehot, axis=1)
    return owned * capacity + placed


def bucketed(entries, slot_of, owners, capacity):
    filled = jnp.full((owners * capacity,), -1, jnp.int32).at[slot_of].set(entries)
    return filled.reshape(owners, capacity)


def look_up_rows(item_table, received):
    present = received >= 0
    looked = item_table[jnp.clip(received, 0)]
    return jnp.where(present[..., None], looked, 0.0)


def local(
    item_table,
    row_accum,
    owner_map,
    row_index,
    bag_index,
    prev_owner,
    prev_row,
    prev_bag,
    grad_pooled,
):
    owners = lax.axis_size("rows")
    rows_dev, width = item_table.shape
    bag_count = grad_pooled.shape[2]
    positions = row_index.shape[2]
    capacity = max(2, 3 * positions // owners)
    bag_range = jnp.arange(bag_count)
    row_range = jnp.arange(rows_dev)
    highest = lax.Precision.HIGHEST
    slot_of = slot_numbers(owner_map[0, 0], owners, capacity)
    send_rows = bucketed(row_index[0, 0], slot_of, owners, capacity)
    send_bags = bucketed(bag_index[0, 0], slot_of, owners, capacity)
    got_rows = lax.all_to_all(send_rows, "rows", split_axis=0, concat_axis=0, tiled=True)
    looked = look_up_rows(item_table, got_rows)
    returned = lax.all_to_all(looked, "rows", split_axis=0, concat_axis=0, tiled=True)
    member = (send_bags[..., None] == bag_range).astype(jnp.float32)
    pooled = jnp.einsum("scb,sce->be", member, returned, precision=highest)
    prev_slots = slot_numbers(prev_owner[0, 0], owners, capacity)
    old_rows = bucketed(prev_row[0, 0], prev_slots, owners, capacity)
    old_bags = bucketed(prev_bag[0, 0], prev_slots, owners, capacity)
    grad_table = grad_pooled[0, 0]
    old_member = (old_bags[..., None] == bag_range).astype(jnp.float32)
    grad_each = jnp.einsum("scb,be->sce", old_member, grad_table, precision=highest)
    got_old_rows = lax.all_to_all(old_rows, "rows", split_axis=0, concat_axis=0, tiled=True)
    got_grads = lax.all_to_all(grad_each, "rows", split_axis=0, concat_axis=0, tiled=True)
    row_hits = (got_old_rows[..., None] == row_range).astype(jnp.float32)
    local_grad = jnp.einsum("scr,sce->re", row_hits, got_grads, precision=highest)
    grad_rows = lax.psum(local_grad, "dp")
    new_accum = row_accum + jnp.mean(grad_rows * grad_rows, axis=1)
    new_table = item_table - learn_rate * grad_rows / jnp.sqrt(new_accum)[:, None]
    return (pooled[None, None], new_table, new_accum)


def solution(mesh):
    placed = (
        P("rows", None),
        P("rows"),
        P("dp", "rows", None, None),
        P("dp", "rows", None),
        P("dp", "rows", None),
        P("dp", "rows", None, None),
        P("dp", "rows", None),
        P("dp", "rows", None),
        P("dp", "rows", None, None),
    )
    return jax.shard_map(
        local,
        mesh=mesh,
        in_specs=placed,
        out_specs=(P("dp", "rows", None, None), P("rows", None), P("rows")),
        check_vma=False,
    )
```

profile of v0, /device:TPU:1, one launch (start us, length us, event | category | flops | bytes accessed | tf_op | source)
XLA Modules:
  0.0 322.5 jit_solution(16624860317048669921)
XLA Ops:
  7.2 0.7 fusion.13
  7.9 1.2 reduce-window.14
  9.1 0.2 slice_reduce_fusion.1
  9.4 0.8 fusion.12
  10.2 0.7 compare_select_fusion.1
  10.9 2.6 scatter_custom_fusion.1
  13.5 0.7 all_to_all.18
  14.2 22.8 %all-to-all-start = ((s32[64,1,24]{2,1,0:T(1,128)}), s32[64,1,24]{2,1,0:T(1,128)S(1)}, u32[]{:S(2)}, u32[]{:S(2)}) async-start(s32[64,1,24]{2,1,0:T(1,128)} %bitcast.8), calls=%async_computation | async-start | bytes 65536 | tf_op jit(solution)/shard_map/all_to_all | solution.py:49
  37.0 0.7 fusion.14
  37.7 1.2 reduce-window.16
  39.1 0.8 fusion.10
  39.9 0.7 compare_select_fusion
  40.6 2.6 scatter_custom_fusion.3
  43.4 2.6 scatter_custom_fusion.2
  46.0 0.7 all_to_all.21
  46.9 3.5 %all-to-all-done = s32[64,1,24]{2,1,0:T(1,128)S(1)} async-done(((s32[64,1,24]{2,1,0:T(1,128)}), s32[64,1,24]{2,1,0:T(1,128)S(1)}, u32[]{:S(2)}, u32[]{:S(2)}) %all-to-all-start) | async-done | bytes 6176 | tf_op jit(solution)/shard_map/all_to_all | solution.py:49
  50.3 11.1 %all-to-all-start.2 = ((s32[64,1,24]{2,1,0:T(1,128)}), s32[64,1,24]{2,1,0:T(1,128)S(1)}, u32[]{:S(2)}, u32[]{:S(2)}) async-start(s32[64,1,24]{2,1,0:T(1,128)} %bitcast.20), calls=%async_computation.2 | async-start | bytes 65536 | tf_op jit(solution)/shard_map/all_to_all | solution.py:60
  61.4 2.0 fusion.16
  63.5 11.6 %all-to-all-done.2 = s32[64,1,24]{2,1,0:T(1,128)S(1)} async-done(((s32[64,1,24]{2,1,0:T(1,128)}), s32[64,1,24]{2,1,0:T(1,128)S(1)}, u32[]{:S(2)}, u32[]{:S(2)}) %all-to-all-start.2) | async-done | bytes 6176 | tf_op jit(solution)/shard_map/all_to_all | solution.py:60
  75.0 5.5 %all-to-all-start.3 = ((f32[64,24,256]{2,1,0:T(8,128)}), f32[64,24,256]{2,1,0:T(8,128)}, u32[]{:S(2)}, u32[]{:S(2)}) async-start(f32[64,24,256]{2,1,0:T(8,128)} %fusion.16), calls=%async_computation.3 | async-start | bytes 3145728 | tf_op jit(solution)/shard_map/all_to_all | solution.py:61
  80.9 4.6 %gather_fusion = f32[1536,256]{1,0:T(8,128)} fusion(f32[2048,256]{1,0:T(8,128)S(1)} %copy-done.1, s32[2048]{0:T(1024)S(1)} %pad_clamp_fusion), kind=kCustom, calls=%fused_computation | custom fusion | bytes 3151872 | tf_op jit(solution)/shard_map/gather | solution.py:23
  85.6 2.8 broadcast_select_fusion
  88.4 63.3 %all-to-all-done.3 = f32[64,24,256]{2,1,0:T(8,128)} async-done(((f32[64,24,256]{2,1,0:T(8,128)}), f32[64,24,256]{2,1,0:T(8,128)}, u32[]{:S(2)}, u32[]{:S(2)}) %all-to-all-start.3) | async-done | bytes 1572896 | tf_op jit(solution)/shard_map/all_to_all | solution.py:61
  151.7 10.3 %all-to-all-start.1 = ((f32[64,24,256]{2,1,0:T(8,128)}), f32[64,24,256]{2,1,0:T(8,128)}, u32[]{:S(2)}, u32[]{:S(2)}) async-start(f32[64,24,256]{2,1,0:T(8,128)} %broadcast_select_fusion), calls=%async_computation.1 | async-start | bytes 3145728 | tf_op jit(solution)/shard_map/all_to_all | solution.py:51
  162.3 13.2 %fusion.2 = f32[2048,256]{1,0:T(8,128)} fusion(s32[64,24]{0,1:T(8,128)S(1)} %copy.38, f32[64,24,256]{2,1,0:T(8,128)} %all-to-all-done.3), kind=kOutput, calls=%fused_computation.8 | convolution fusion | flops 9666822144 | bytes 3676160 | tf_op jit(solution)/shard_map/scr,sce->re/dot_general | solution.py:63
  175.6 2.6 scatter_custom_fusion
  178.3 55.0 %all-to-all-done.1 = f32[64,24,256]{2,1,0:T(8,128)} async-done(((f32[64,24,256]{2,1,0:T(8,128)}), f32[64,24,256]{2,1,0:T(8,128)}, u32[]{:S(2)}, u32[]{:S(2)}) %all-to-all-start.1) | async-done | bytes 1572896 | tf_op jit(solution)/shard_map/all_to_all | solution.py:51
  233.4 3.0 fusion.6
  236.4 74.8 %all-reduce.2.cloned.1.call-done = f32[2048,256]{1,0:T(8,128)} async-done(((f32[2048,256]{1,0:T(8,128)}), f32[2048,256]{1,0:T(8,128)}) %all-reduce.2.cloned.1.call-update) | async-done | bytes 2097168 | tf_op jit(solution)/shard_map/psum | solution.py:64
  311.2 2.1 multiply_reduce_fusion
  313.3 0.6 fusion.26
  313.9 1.8 divide_subtract_fusion
  (29 shorter events, 1.4 us)
Async XLA Ops:
  7.2 54.3 %copy-start = (f32[1,1,4,256]{3,2,1,0:T(4,128)S(1)}, f32[1,1,4,256]{3,2,1,0:T(4,128)}, u32[]{:S(2)}) copy-start(f32[1,1,4,256]{3,2,1,0:T(4,128)} %param.17) | copy-start | bytes 12292
  14.2 36.2 %all-to-all-start = ((s32[64,1,24]{2,1,0:T(1,128)}), s32[64,1,24]{2,1,0:T(1,128)S(1)}, u32[]{:S(2)}, u32[]{:S(2)}) async-start(s32[64,1,24]{2,1,0:T(1,128)} %bitcast.8), calls=%async_computation | async-start | bytes 65536 | tf_op jit(solution)/shard_map/all_to_all | solution.py:49
  50.3 24.7 %all-to-all-start.2 = ((s32[64,1,24]{2,1,0:T(1,128)}), s32[64,1,24]{2,1,0:T(1,128)S(1)}, u32[]{:S(2)}, u32[]{:S(2)}) async-start(s32[64,1,24]{2,1,0:T(1,128)} %bitcast.20), calls=%async_computation.2 | async-start | bytes 65536 | tf_op jit(solution)/shard_map/all_to_all | solution.py:60
  63.5 17.5 %copy-start.1 = (f32[2048,256]{1,0:T(8,128)S(1)}, f32[2048,256]{1,0:T(8,128)}, u32[]{:S(2)}) copy-start(f32[2048,256]{1,0:T(8,128)} %param.9) | copy-start | bytes 6291460
  75.0 76.7 %all-to-all-start.3 = ((f32[64,24,256]{2,1,0:T(8,128)}), f32[64,24,256]{2,1,0:T(8,128)}, u32[]{:S(2)}, u32[]{:S(2)}) async-start(f32[64,24,256]{2,1,0:T(8,128)} %fusion.16), calls=%async_computation.3 | async-start | bytes 3145728 | tf_op jit(solution)/shard_map/all_to_all | solution.py:61
  151.7 81.6 %all-to-all-start.1 = ((f32[64,24,256]{2,1,0:T(8,128)}), f32[64,24,256]{2,1,0:T(8,128)}, u32[]{:S(2)}, u32[]{:S(2)}) async-start(f32[64,24,256]{2,1,0:T(8,128)} %broadcast_select_fusion), calls=%async_computation.1 | async-start | bytes 3145728 | tf_op jit(solution)/shard_map/all_to_all | solution.py:51
  162.0 149.2 %all-reduce.2.cloned.1.call-start = ((), (), s32[]{:S(2)}) async-start(), calls=%async_computation.4 | async-start | bytes 4194304 | tf_op jit(solution)/shard_map/psum | solution.py:64
  178.3 135.0 %copy-start.3 = (f32[2048]{0:T(1024)S(1)}, f32[2048]{0:T(1024)}, u32[]{:S(2)}) copy-start(f32[2048]{0:T(1024)} %param.10) | copy-start | bytes 24580
  311.2 2.7 copy-start.2
Sparse Core Ops, SparseCore 0:
  175.7 135.4 all-reduce.1
where the time goes:
time: 323 us
  waiting for transfers between devices  208 us (64%)
  starting transfers between devices  49.8 us (15%)
  matrix products  18.3 us (6%)
  local copies, waits for them, and re-layouts  17.8 us (6%)
  other arithmetic  14.2 us (4%)
  between operations  14.2 us (4%)
    psum x1, waiting for transfers between devices, local(): grad_rows = lax.psum(local_grad, 'dp')  74.8 us
    all_to_all x1, waiting for transfers between devices, local(): lax.all_to_all(grad_each, 'rows', split_axis=0, concat_axis=0, tiled=True)  63.3 us
    all_to_all x1, waiting for transfers between devices, local(): lax.all_to_all(looked, 'rows', split_axis=0, concat_axis=0, tiled=True)  55 us
    all_to_all x1, starting transfers between devices, local(): lax.all_to_all(send_rows, 'rows', split_axis=0, concat_axis=0, tiled=True)  22.8 us
    dot_general x1, matrix products, local(): jnp.einsum('scr,sce->re', row_hits, got_grads, precision=highest)  13.2 us
    all_to_all x1, waiting for transfers between devices, local(): lax.all_to_all(old_rows, 'rows', split_axis=0, concat_axis=0, tiled=True)  11.6 us
    all_to_all x1, starting transfers between devices, local(): lax.all_to_all(old_rows, 'rows', split_axis=0, concat_axis=0, tiled=True)  11.1 us
    scatter x4, local copies, waits for them, and re-layouts, bucketed(): jnp.full((owners * capacity,), -1, jnp.int32).at[slot_of].set(entries)  10.4 us
  transfers between devices with their start and end apart: 5, of which 5 were waited for; matrix products, arithmetic and copies ran while one was open for 12% of the time, Pallas kernels for 0%

commit v1 on v0

v1 whole, which is shorter than its diff:
```python
import functools

import jax
import jax.numpy as jnp
from jax import lax
from jax.experimental import pallas as pl
from jax.experimental.pallas import tpu as pltpu
from jax.sharding import PartitionSpec as P

learn_rate = 0.1
CAP = 24
NX = 4
MESH = pl.DeviceIdType.MESH
F32, BF16, I32 = jnp.float32, jnp.bfloat16, jnp.int32
NT = (((1,), (1,)), ((), ()))
NN = (((1,), (0,)), ((), ()))


def dot(a, b, dims=NN):
    return lax.dot_general(a, b, dims, preferred_element_type=F32)


def iota(shape, axis):
    return lax.broadcasted_iota(I32, shape, axis)


def split(v):
    high = v.astype(BF16)
    return high, (v - high.astype(F32)).astype(BF16)


def one_hot(mask):
    return jnp.where(mask, 1.0, 0.0).astype(BF16)


def by_owner(owner, row, bag, powner, prow, pbag, nz):
    n = owner.shape[1]

    def owners(o):
        return iota((nz * 8, n), 0) == (o // NX) * 8 + o % NX

    mine, old = owners(owner), owners(powner)
    both = jnp.concatenate([one_hot(mine), one_hot(old)], axis=0)
    before = one_hot(iota((n, n), 0) < iota((n, n), 1))
    count = dot(both, before)

    def places(mask, count, row, bag):
        rank = jnp.sum(jnp.where(mask, count, 0.0), axis=0, keepdims=True)
        hit = iota((32, n), 0).astype(F32) == rank
        row = row + 1
        low, high, bag = (v.astype(F32) for v in (row % 128, row // 128, bag))
        pick = lambda v: jnp.where(hit, v, 0.0)
        return pick(low), pick(high), pick(bag)

    low, high, bags = places(mine, count[: nz * 8], row, bag)
    plow, phigh, pbags = places(old, count[nz * 8:], prow, pbag)
    none, none2 = jnp.zeros((64, n), F32), jnp.zeros((32, n), F32)
    cat = functools.partial(jnp.concatenate, axis=0)
    lows = jnp.concatenate([cat([low, bags, none]), cat([none, plow, pbags])], axis=1)
    highs = jnp.concatenate([cat([high, none2, none]), cat([none, phigh, none2])], axis=1)
    left = jnp.concatenate([both[: nz * 8], both[nz * 8:]], axis=1)
    return dot(left, lows.astype(BF16), NT) + 128.0 * dot(left, highs.astype(BF16), NT)


def kernel(
    ny, nz,
    owner, row, bag, powner, prow, pbag, grad, accum, table,
    pooled, new_table, new_accum,
    tab, tabs, zsend, zbuf, xsend, xbuf, expand, hits, look, part, psend, pbuf, qsend, qbuf,
    u, rbuf, gall, tout, nacc,
    tab_sem, out_sem, z_sem, x_send, x_recv, c_send, c_recv,
    rs_send, rs_recv, ag_send, ag_recv, k_send, k_recv, px_send, px_recv, pz_sem,
):
    dp, rw = lax.axis_index("dp"), lax.axis_index("rows")
    y, c, z, x = dp // 2, dp % 2, rw // NX, rw % NX
    ns = NX * nz
    rows_dev = tab.shape[0]
    half_rows = rows_dev // 2
    nb = half_rows // ny
    nh = nb // 2
    gt = nz * 8

    def at(dp_, rw_):
        return {"dp": dp_, "rows": rw_}

    def z_peer(d):
        return at(dp, ((z + d) % nz) * NX + x)

    def x_peer(d):
        return at(dp, z * NX + (x + d) % NX)

    partner = at(y * 2 + 1 - c, rw)
    y_peer = [at(((y + 1) % ny) * 2 + c, rw), at(((y + ny - 1) % ny) * 2 + c, rw)]

    def remote(src, dst, s, r, dev):
        return pltpu.make_async_remote_copy(
            src_ref=src, dst_ref=dst, send_sem=s, recv_sem=r, device_id=dev, device_id_type=MESH
        )

    load = pltpu.make_async_copy(table, tab, tab_sem)
    load.start()
    barrier = pltpu.get_barrier_semaphore()

    def greet(d, _):
        pl.semaphore_signal(barrier, inc=1, device_id=z_peer(d), device_id_type=MESH)
        return 0

    lax.fori_loop(1, nz, greet, 0)
    for d in range(1, NX):
        pl.semaphore_signal(barrier, inc=1, device_id=x_peer(d), device_id_type=MESH)
    for dev in [partner] + y_peer:
        pl.semaphore_signal(barrier, inc=1, device_id=dev, device_id_type=MESH)

    message = by_owner(
        owner[...], row[...], bag[...], powner[...], prow[...], pbag[...], nz
    )
    g4 = grad[...]
    tile = jnp.concatenate([g4[:, :128], g4[:, 128:]], axis=0)
    for i in range(nz):
        zsend[i, 0:8, :] = tile
        zsend[i, 8:16, :] = message[i * 8:(i + 1) * 8]
    pl.semaphore_wait(barrier, nz - 1 + NX - 1 + 1 + 2)

    def send_z(d, _):
        to = (z + d) % nz
        remote(zsend.at[to], zbuf.at[z], z_sem.at[0], z_sem.at[1], z_peer(d)).start()
        return 0

    lax.fori_loop(1, nz, send_z, 0)
    zbuf[z] = zsend[z]
    others = zbuf.at[pl.ds(0, nz - 1)]
    z_all = remote(others, others, z_sem.at[0], z_sem.at[1], z_peer(1))
    z_all.wait_recv()

    for i in range(NX):
        for j in range(nz):
            xsend[i, j * 8:(j + 1) * 8, :] = zbuf[j, 0:8, :]
        xsend[i, gt:gt + nz, :] = zbuf[:, 8 + i, :]
    x_copies = []
    for d in range(1, NX):
        x_copies.append(
            remote(xsend.at[(x + d) % NX], xbuf.at[c, x], x_send.at[d], x_recv.at[d], x_peer(d))
        )
        x_copies[-1].start()
    xbuf[c, x] = xsend[x]
    c_copies = []
    for d in range(NX):
        if d > 0:
            x_copies[d - 1].wait_recv()
        piece = xbuf.at[c, (x + NX - d) % NX]
        c_copies.append(remote(piece, piece, c_send.at[d], c_recv.at[d], partner))
        c_copies[-1].start()

    load.wait()
    high, low = split(tab[...])
    tabs[:, 0:256] = high
    tabs[:, 256:512] = low
    for copy in c_copies:
        copy.wait_recv()

    ids = jnp.concatenate([xbuf[i, j, gt:gt + nz, :] for i in range(2) for j in range(NX)], axis=0)
    lines = 2 * ns
    grads = []
    for b in range(4):
        sides = [
            jnp.concatenate(
                [
                    xbuf[i, j, pl.ds(b + 4 * h, nz, stride=8), :]
                    for i in range(2)
                    for j in range(NX)
                ],
                axis=0,
            )
            for h in range(2)
        ]
        grads.append(jnp.concatenate(sides, axis=1))
    for k in range(CAP):
        of = ids[:, 96 + k:97 + k]
        each = jnp.where(of < 0.5, grads[0], jnp.where(of < 1.5, grads[1], jnp.where(of < 2.5, grads[2], grads[3])))
        high, low = split(each)
        expand[k * lines:(k + 1) * lines, 0:256] = high
        expand[k * lines:(k + 1) * lines, 256:512] = low
    keys = ids.T[64:64 + CAP]

    def sums(offsets):
        for i, d in enumerate(offsets):
            base = c * half_rows + ((y + d + ny) % ny) * nb + 1
            number = (iota((nb, lines), 0) + base).astype(F32)
            for k in range(CAP):
                hits[i * nb:(i + 1) * nb, k * lines:(k + 1) * lines] = one_hot(number == keys[k:k + 1, :])
        both = dot(hits[...], expand[...])
        total = both[:, 0:256] + both[:, 256:512]
        for i, d in enumerate(offsets):
            u[(d + ny) % ny] = total[i * nb:(i + 1) * nb]

    mine = jnp.concatenate([xbuf[c, j, gt:gt + nz, :] for j in range(NX)], axis=0)
    slots = CAP // 3

    def look_up(first):
        for k in range(slots):
            col = mine[:, first + k:first + k + 1]
            number = (iota((ns, rows_dev), 1) + 1).astype(F32)
            look[k * ns:(k + 1) * ns, :] = one_hot(number == col)
        both = dot(look[...], tabs[...])
        found = both[:, 0:256] + both[:, 256:512]
        for b in range(4):
            total = jnp.zeros((ns, 256), F32) if first == 0 else part[b]
            for k in range(slots):
                of = mine[:, 32 + first + k:33 + first + k]
                total = total + jnp.where(of == b, found[k * ns:(k + 1) * ns], 0.0)
            part[b] = total

    def cut(ref, h):
        return ref.at[pl.ds(h * nh, nh)]

    half = ny // 2
    pieces = [(1, 0)] + [(t, h) for t in range(2, half + 1) for h in (1, 0)]
    number_of = {piece: i for i, piece in enumerate(pieces)}
    rs_copies = {}

    def rs_copy(way, t, h):
        i = number_of[(t, h)]
        d = half + 1 - t
        src = cut(u.at[d if way == 0 else (ny - d) % ny], h if way == 0 else 1 - h)
        copy = remote(src, rbuf.at[way, i], rs_send.at[way, i], rs_recv.at[way, i], y_peer[way])
        rs_copies[way, t, h] = copy
        copy.start()

    def rs_take(way, t, h):
        rs_copies[way, t, h].wait_recv()
        i = number_of[(t, h)]
        d = half - t
        hh = h if way == 0 else 1 - h
        slot = d if way == 0 else (ny - d) % ny
        rows = pl.ds(hh * nh, nh)
        u[slot, rows, :] = u[slot, rows, :] + rbuf[way, i]

    sums((half, 0))
    for way in range(2):
        rs_copy(way, 1, 0)
    pool_steps = 0
    for t in range(2, half + 1):
        d = half + 1 - t
        sums((d, -d))
        for way in range(2):
            if t == 2:
                rs_copy(way, t, 1)
        for h in (1, 0) if t > 2 else (0,):
            for way in range(2):
                rs_take(way, t - 1, h)
                rs_copy(way, t, h)
        if pool_steps < 3:
            look_up(pool_steps * slots)
            pool_steps += 1
    while pool_steps < 3:
        look_up(pool_steps * slots)
        pool_steps += 1

    for b in range(4):
        total = part[b]
        for h in range(2):
            psend[pl.ds(b + 4 * h, ns, stride=8), :] = total[:, h * 128:(h + 1) * 128]
    px_copies = []
    for d in range(1, NX):
        src = psend.at[pl.ds(((x + d) % NX) * gt, gt)]
        px_copies.append(remote(src, pbuf.at[d], px_send.at[d], px_recv.at[d], x_peer(d)))
        px_copies[-1].start()

    for h in (1, 0):
        for way in range(2):
            rs_take(way, half, h)

    def block(line, core, h):
        return pl.ds(core * half_rows + line * nb + h * nh, nh)

    def from_line(way, t):
        return (y + ny - t) % ny if way == 0 else (y + t) % ny

    ag_copies, k_copies = {}, {}

    def ag_copy(way, t, h):
        rows = gall.at[block(from_line(way, t - 1), c, h)]
        i = (t - 1) * 2 + h
        ag_copies[way, t, h] = remote(rows, rows, ag_send.at[way, i], ag_recv.at[way, i], y_peer[way])
        ag_copies[way, t, h].start()

    def core_copy(way, t, h):
        rows = gall.at[block(from_line(way, t), c, h)]
        i = t * 2 + h
        k_copies[way, t, h] = remote(rows, rows, k_send.at[way, i], k_recv.at[way, i], partner)
        k_copies[way, t, h].start()

    def goes(way, t, h):
        return t < half or (t == half and h == way)

    for h in range(2):
        gall[block(y, c, h), :] = u[0, h * nh:(h + 1) * nh, :]
    for h in range(2):
        for way in range(2):
            if goes(way, 1, h if way == 0 else 1 - h):
                ag_copy(way, 1, h if way == 0 else 1 - h)
    for h in range(2):
        core_copy(0, 0, h)

    out_copies = []

    def update(way, t, h, core):
        line = from_line(way, t)
        rows = block(line, core, h)
        g = gall[rows, :]
        at_row = core * ny + line
        eye = iota((nh, nb), 0) + h * nh == iota((nh, nb), 1)
        before = jnp.sum(jnp.where(eye, accum[pl.ds(at_row, 1), :], 0.0), axis=1, keepdims=True)
        after = before + jnp.sum(g * g, axis=1, keepdims=True) * (1.0 / g.shape[1])
        tout[rows, :] = tab[rows, :] - learn_rate * g / jnp.sqrt(after)
        nacc[h, pl.ds(at_row, 1), :] = jnp.sum(jnp.where(eye, after, 0.0), axis=0, keepdims=True)
        pltpu.make_async_copy(tout.at[rows], new_table.at[rows], out_sem).start()

    for h in range(2):
        update(0, 0, h, c)

    for copy in px_copies:
        copy.wait_recv()
    total = psend[pl.ds(x * gt, gt), :]
    for d in range(1, NX):
        total = total + pbuf[d]
    for i in range(nz):
        qsend[i] = total[i * 8:(i + 1) * 8]

    def send_q(d, _):
        to = (z + d) % nz
        remote(qsend.at[to], qbuf.at[z], pz_sem.at[0], pz_sem.at[1], z_peer(d)).start()
        return 0

    lax.fori_loop(1, nz, send_q, 0)
    qbuf[z] = qsend[z]

    late = [(0, 0, 0), (0, 0, 1)]
    for t in range(1, half + 1):
        came = []
        for h in range(2):
            for way in range(2):
                hh = h if way == 0 else 1 - h
                if goes(way, t, hh):
                    ag_copies[way, t, hh].wait_recv()
                    if goes(way, t + 1, hh):
                        ag_copy(way, t + 1, hh)
                    core_copy(way, t, hh)
                    came.append((way, t, hh))
        for way, tt, h in came:
            update(way, tt, h, c)
        for way, tt, h in late:
            k_copies[way, tt, h].wait_recv()
            update(way, tt, h, 1 - c)
        late = came
    q_others = qbuf.at[pl.ds(0, nz - 1)]
    q_all = remote(q_others, q_others, pz_sem.at[0], pz_sem.at[1], z_peer(1))
    q_all.wait_recv()
    total = qbuf[0]
    for i in range(1, nz):
        total = total + qbuf[i]
    pooled[:, 0:128] = total[0:4]
    pooled[:, 128:256] = total[4:8]
    for way, tt, h in late:
        k_copies[way, tt, h].wait_recv()
        update(way, tt, h, 1 - c)
    new_accum[...] = nacc[0] + nacc[1]

    pltpu.make_async_copy(tout, new_table, out_sem).wait()
    z_all.wait_send()
    q_all.wait_send()
    for copy in x_copies + c_copies + px_copies:
        copy.wait_send()
    for copies in (rs_copies, ag_copies, k_copies):
        for copy in copies.values():
            copy.wait_send()


def local(
    ny, nz,
    item_table, row_accum, owner_map, row_index, bag_index, prev_owner, prev_row, prev_bag, grad_pooled,
):
    rows_dev, width = item_table.shape
    bags = grad_pooled.shape[2]
    n = row_index.shape[2]
    half_rows = rows_dev // 2
    nb = half_rows // ny
    nh = nb // 2
    ns, gt, half = NX * nz, nz * 8, ny // 2
    lines = 2 * ns
    line = lambda a: a.reshape(1, n)
    vmem = pl.BlockSpec(memory_space=pltpu.VMEM)
    hbm = pl.BlockSpec(memory_space=pl.ANY)
    dma = pltpu.SemaphoreType.DMA
    pooled, new_table, new_accum = pl.pallas_call(
        functools.partial(kernel, ny, nz),
        out_shape=[
            jax.ShapeDtypeStruct((bags, width), F32),
            jax.ShapeDtypeStruct((rows_dev, width), F32),
            jax.ShapeDtypeStruct((rows_dev // nb, nb), F32),
        ],
        in_specs=[vmem] * 8 + [hbm],
        out_specs=[vmem, hbm, vmem],
        scratch_shapes=[
            pltpu.VMEM((rows_dev, width), F32),
            pltpu.VMEM((rows_dev, 2 * width), BF16),
            pltpu.VMEM((nz, 16, 128), F32),
            pltpu.VMEM((nz, 16, 128), F32),
            pltpu.VMEM((NX, gt + nz, 128), F32),
            pltpu.VMEM((2, NX, gt + nz, 128), F32),
            pltpu.VMEM((CAP * lines, 2 * width), BF16),
            pltpu.VMEM((2 * nb, CAP * lines), BF16),
            pltpu.VMEM((CAP // 3 * ns, rows_dev), BF16),
            pltpu.VMEM((4, ns, width), F32),
            pltpu.VMEM((ns * 8, 128), F32),
            pltpu.VMEM((NX, gt, 128), F32),
            pltpu.VMEM((nz, 8, 128), F32),
            pltpu.VMEM((nz, 8, 128), F32),
            pltpu.VMEM((ny, nb, width), F32),
            pltpu.VMEM((2, 2 * half - 1, nh, width), F32),
            pltpu.VMEM((rows_dev, width), F32),
            pltpu.VMEM((rows_dev, width), F32),
            pltpu.VMEM((2, rows_dev // nb, nb), F32),
            dma(()), dma(()), dma((2,)),
            dma((NX,)), dma((NX,)), dma((NX,)), dma((NX,)),
            dma((2, 2 * half)), dma((2, 2 * half)),
            dma((2, 2 * half)), dma((2, 2 * half)),
            dma((2, 2 * half + 2)), dma((2, 2 * half + 2)),
            dma((NX,)), dma((NX,)), dma((2,)),
        ],
        compiler_params=pltpu.CompilerParams(
            collective_id=0, has_side_effects=True, vmem_limit_bytes=56 * 1024 * 1024
        ),
    )(
        line(owner_map), line(row_index), line(bag_index),
        line(prev_owner), line(prev_row), line(prev_bag),
        grad_pooled.reshape(bags, width), row_accum.reshape(rows_dev // nb, nb), item_table,
    )
    return (
        pooled.reshape(1, 1, bags, width),
        new_table,
        new_accum.reshape(rows_dev),
    )


def solution(mesh):
    ny, nz = mesh.shape["dp"] // 2, mesh.shape["rows"] // NX
    placed = (
        P("rows", None),
        P("rows"),
        P("dp", "rows", None, None),
        P("dp", "rows", None),
        P("dp", "rows", None),
        P("dp", "rows", None, None),
        P("dp", "rows", None),
        P("dp", "rows", None),
        P("dp", "rows", None, None),
    )
    return jax.shard_map(
        functools.partial(local, ny, nz),
        mesh=mesh,
        in_specs=placed,
        out_specs=(P("dp", "rows", None, None), P("rows", None), P("rows")),
        check_vma=False,
    )
```

time: 323 us -> 85 us (0.26)
  waiting for transfers between devices: 208 us -> 0 us
  Pallas kernels: 0 us -> 78.6 us
  starting transfers between devices: 49.8 us -> 0 us
  matrix products: 18.3 us -> 0 us
  other arithmetic: 14.2 us -> 0 us
  between operations: 14.2 us -> 0.64 us
  local copies, waits for them, and re-layouts: 17.8 us -> 4.93 us
    all_to_all x4 -> x0, waiting for transfers between devices: 133 us -> none  [the longest x1 63.3 us: local(): lax.all_to_all(grad_each, 'rows', split_axis=0, concat_axis=0, tiled=True)]
    pallas_call x0 -> x1, Pallas kernels: none -> 78.6 us  [local(): pl.pallas_call(functools.partial(kernel, ny, nz), out_shape=[jax.ShapeDty...]
    psum x1 -> x0, waiting for transfers between devices: 74.8 us -> none  [local(): grad_rows = lax.psum(local_grad, 'dp')]
    all_to_all x4 -> x0, starting transfers between devices: 49.6 us -> none  [the longest x1 22.8 us: local(): lax.all_to_all(send_rows, 'rows', split_axis=0, concat_axis=0, tiled=True)]
    dot_general x3 -> x0, matrix products: 18.3 us -> none  [the longest x1 13.2 us: local(): jnp.einsum('scr,sce->re', row_hits, got_grads, precision=highest)]
    scatter x4 -> x0, local copies, waits for them, and re-layouts: 10.4 us -> none  [bucketed(): jnp.full((owners * capacity,), -1, jnp.int32).at[slot_of].set(entries)]
    unnamed x8 -> x5, local copies, waits for them, and re-layouts: 0.02 us -> 4.93 us
    gather x1 -> x0, local copies, waits for them, and re-layouts: 4.64 us -> none  [look_up_rows(): looked = item_table[jnp.clip(received, 0)]]
  transfers between devices with their start and end apart: 5 -> 0, of which waited for: 5 -> 0; matrix products, arithmetic and copies ran while one was open for 12% -> 0% of each run, Pallas kernels for 0% -> 0%
where the time goes in v1:
time: 85 us; the launch traced here: 84.1 us
  Pallas kernels  78.6 us (92%)
  local copies, waits for them, and re-layouts  4.93 us (6%)
    pallas_call x1, Pallas kernels, local(): pl.pallas_call(functools.partial(kernel, ny, nz), out_shape=[jax.ShapeDty...  78.6 us
    unnamed x5, local copies, waits for them, and re-layouts  4.93 us

profile of v1, /device:TPU:1, one launch (start us, length us, event | category | flops | bytes accessed | tf_op | source)
XLA Modules:
  0.0 84.1 jit_solution(11624737579100488825)
XLA Ops:
  0.6 78.6 %shard_map.112 = (f32[4,256]{1,0:T(4,128)}, f32[2048,256]{1,0:T(8,128)}, f32[16,128]{1,0:T(8,128)}) custom-call(s32[1,512]{1,0:T(1,128)} %bitcast.14, s32[1,512]{1,0:T(1,128)} %bitcast.15, s32[1,512]{1,0:T(1,128)} %bitcast.16, s32[1,512]{1,0:T(1,128)} %bitcast.17, s32[1,512]{1,0:T(1,128)} %bitcast.18, s32[1,512]{1,0:T(1,128)} %bitcast.19, ...), custom_call_target="tpu_custom_call" | custom-call | tf_op jit(solution)/shard_map/pallas_call | solution.py:395
  79.2 1.3 %copy.15 = f32[1,1,4,256]{3,2,1,0:T(4,128)} copy(f32[1,1,4,256]{3,2,1,0:T(4,128)} %bitcast.13) | data formatting | bytes 8192
  80.5 0.0 copy-start
  80.5 3.1 %copy.16 = f32[2048,256]{1,0:T(8,128)} copy(f32[2048,256]{1,0:T(8,128)} %get-tuple-element.13) | data formatting | bytes 4194304
  83.5 0.0 copy-done
  83.5 0.6 copy.17
Async XLA Ops:
  80.5 3.1 %copy-start = (f32[16,128]{1,0:T(8,128)S(1)}, f32[16,128]{1,0:T(8,128)}, u32[]{:S(2)}) copy-start(f32[16,128]{1,0:T(8,128)} %get-tuple-element.8) | copy-start | bytes 24580

commit v2 on v1

v2 whole, which is shorter than its diff:
```python
import functools

import jax
import jax.numpy as jnp
from jax import lax
from jax.experimental import pallas as pl
from jax.experimental.pallas import tpu as pltpu
from jax.sharding import PartitionSpec as P

learn_rate = 0.1
CAP = 24
NX = 4
MESH = pl.DeviceIdType.MESH
F32, BF16, I32 = jnp.float32, jnp.bfloat16, jnp.int32
NT = (((1,), (1,)), ((), ()))
NN = (((1,), (0,)), ((), ()))


def dot(a, b, dims=NN):
    return lax.dot_general(a, b, dims, preferred_element_type=F32)


def iota(shape, axis):
    return lax.broadcasted_iota(I32, shape, axis)


def split(v):
    high = v.astype(BF16)
    return high, (v - high.astype(F32)).astype(BF16)


def one_hot(mask):
    return jnp.where(mask, 1.0, 0.0).astype(BF16)


def by_owner(owner, row, bag, powner, prow, pbag, nz):
    n = owner.shape[1]

    def owners(o):
        return iota((nz * 8, n), 0) == (o // NX) * 8 + o % NX

    now, old = owners(owner), owners(powner)
    before = one_hot(iota((n, n), 0) < iota((n, n), 1))
    count = dot(jnp.concatenate([one_hot(now), one_hot(old)], axis=0), before)

    def places(mask, count, row, bag):
        rank = jnp.sum(jnp.where(mask, count, 0.0), axis=0, keepdims=True)
        hit = iota((32, n), 0).astype(F32) == rank
        row = row + 1
        low, high, bag = (v.astype(F32) for v in (row % 128, row // 128, bag))
        pick = lambda v: jnp.where(hit, v, 0.0)
        return [pick(low), pick(bag)], [pick(high), jnp.zeros((32, n), F32)]

    none = [jnp.zeros((64, n), F32)]
    left, lows, highs = [], [], []
    for o, first, (low, high) in (
        (powner, 0, places(old, count[nz * 8:], prow, pbag)),
        (owner, 2, places(now, count[: nz * 8], row, bag)),
    ):
        x = o % NX
        line = (o // NX) * 8 + first + x // 2
        for side in range(2):
            left.append(one_hot((iota((nz * 8, n), 0) == line) & (x % 2 == side)))
            fill = lambda v: jnp.concatenate(v + none if side == 0 else none + v, axis=0)
            lows.append(fill(low).astype(BF16))
            highs.append(fill(high).astype(BF16))
    left, lows, highs = (jnp.concatenate(v, axis=1) for v in (left, lows, highs))
    return dot(left, lows, NT) + 128.0 * dot(left, highs, NT)


def kernel(
    ny, nz,
    owner, row, bag, powner, prow, pbag, grad, accum, table,
    pooled, new_table, new_accum,
    idbuf, gradbuf, accbuf, in_sem, tab, tabs, zsend, zbuf, z2send, z2buf, xsend, xbuf, x2send, x2buf,
    expand, hits, look, part, psend, pbuf, qsend, qbuf, u, rbuf, gall,
    tab_sem, z_sem, z2_sem, x_send, x_recv, x2_send, x2_recv, c_send, c_recv,
    rs_send, rs_recv, ag_send, ag_recv, k_send, k_recv, px_send, px_recv, pz_sem,
):
    dp, rw = lax.axis_index("dp"), lax.axis_index("rows")
    y, c, z, x = dp // 2, dp % 2, rw // NX, rw % NX
    ns = NX * nz
    rows_dev = tab.shape[0]
    half_rows = rows_dev // 2
    nb = half_rows // ny
    nh = nb // 2
    gt = nz * 8

    def at(dp_, rw_):
        return {"dp": dp_, "rows": rw_}

    def far_first(i):
        return nz // 2 + (i % 2) * ((i + 1) // 2) - (1 - i % 2) * (i // 2)

    def z_peer(d):
        return at(dp, ((z + d) % nz) * NX + x)

    def x_peer(d):
        return at(dp, z * NX + (x + d) % NX)

    partner = at(y * 2 + 1 - c, rw)
    y_peer = [at(((y + 1) % ny) * 2 + c, rw), at(((y + ny - 1) % ny) * 2 + c, rw)]

    def remote(src, dst, s, r, dev):
        return pltpu.make_async_remote_copy(
            src_ref=src, dst_ref=dst, send_sem=s, recv_sem=r, device_id=dev, device_id_type=MESH
        )

    barrier = pltpu.get_barrier_semaphore()

    def greet(i, _):
        pl.semaphore_signal(barrier, inc=1, device_id=z_peer(far_first(i)), device_id_type=MESH)
        return 0

    lax.fori_loop(0, nz - 1, greet, 0)
    for d in range(1, NX):
        pl.semaphore_signal(barrier, inc=1, device_id=x_peer(d), device_id_type=MESH)
    for dev in [partner] + y_peer:
        pl.semaphore_signal(barrier, inc=1, device_id=dev, device_id_type=MESH)

    firsts = [
        pltpu.make_async_copy(src, idbuf.at[i], in_sem.at[i])
        for i, src in enumerate((powner, prow, pbag, owner, row, bag))
    ]
    firsts.append(pltpu.make_async_copy(grad, gradbuf, in_sem.at[6]))
    for copy in firsts:
        copy.start()
    loads = [
        pltpu.make_async_copy(accum, accbuf, in_sem.at[7]),
        pltpu.make_async_copy(table, tab, tab_sem),
    ]
    for copy in loads:
        copy.start()
    for copy in firsts:
        copy.wait()
    message = by_owner(
        idbuf[3], idbuf[4], idbuf[5], idbuf[0], idbuf[1], idbuf[2], nz
    )
    g4 = gradbuf[...]
    tile = jnp.concatenate([g4[:, :128], g4[:, 128:]], axis=0)
    for i in range(nz):
        zsend[i, 0:8, :] = tile
        zsend[i, 8:10, :] = message[i * 8:i * 8 + 2]
        z2send[i] = message[i * 8 + 2:i * 8 + 4]
    pl.semaphore_wait(barrier, nz - 1 + NX - 1 + 1 + 2)

    def send_z(i, _):
        d = far_first(i)
        to = (z + d) % nz
        remote(zsend.at[to], zbuf.at[z], z_sem.at[0], z_sem.at[1], z_peer(d)).start()
        return 0

    def send_z2(i, _):
        d = far_first(i)
        to = (z + d) % nz
        remote(z2send.at[to], z2buf.at[z], z2_sem.at[0], z2_sem.at[1], z_peer(d)).start()
        return 0

    def from_others(buf, sems):
        others = buf.at[pl.ds(0, nz - 1)]
        return remote(others, others, sems.at[0], sems.at[1], z_peer(1))

    lax.fori_loop(0, nz - 1, send_z, 0)
    lax.fori_loop(0, nz - 1, send_z2, 0)
    zbuf[z] = zsend[z]
    z2buf[z] = z2send[z]
    z_all, z2_all = from_others(zbuf, z_sem), from_others(z2buf, z2_sem)
    z_all.wait_recv()

    for i in range(NX):
        for j in range(nz):
            xsend[i, j * 8:(j + 1) * 8, :] = zbuf[j, 0:8, :]
        xsend[i, gt:gt + nz, :] = zbuf[:, 8 + i // 2, :]
    x_copies = []
    for d in range(1, NX):
        x_copies.append(
            remote(xsend.at[(x + d) % NX], xbuf.at[c, x], x_send.at[d], x_recv.at[d], x_peer(d))
        )
        x_copies[-1].start()
    xbuf[c, x] = xsend[x]
    own = xbuf.at[c, x]
    c_copies = [remote(own, own, c_send.at[0], c_recv.at[0], partner)]
    c_copies[0].start()
    z2_all.wait_recv()
    for i in range(NX):
        x2send[i] = z2buf[:, i // 2, :]
    x2_copies = []
    for d in range(1, NX):
        x2_copies.append(
            remote(x2send.at[(x + d) % NX], x2buf.at[x], x2_send.at[d], x2_recv.at[d], x_peer(d))
        )
        x2_copies[-1].start()
    x2buf[x] = x2send[x]
    for d in range(1, NX):
        x_copies[d - 1].wait_recv()
        piece = xbuf.at[c, (x + NX - d) % NX]
        c_copies.append(remote(piece, piece, c_send.at[d], c_recv.at[d], partner))
        c_copies[-1].start()

    for copy in loads:
        copy.wait()
    high, low = split(tab[...])
    tabs[:, 0:256] = high
    tabs[:, 256:512] = low
    for copy in c_copies:
        copy.wait_recv()

    def own_lanes(v):
        return jnp.where(x % 2 == 0, v, pltpu.roll(v, 64, 1))

    ids = own_lanes(
        jnp.concatenate([xbuf[i, j, gt:gt + nz, :] for i in range(2) for j in range(NX)], axis=0)
    )
    lines = 2 * ns
    grads = []
    for b in range(4):
        sides = [
            jnp.concatenate(
                [
                    xbuf[i, j, pl.ds(b + 4 * h, nz, stride=8), :]
                    for i in range(2)
                    for j in range(NX)
                ],
                axis=0,
            )
            for h in range(2)
        ]
        grads.append(jnp.concatenate(sides, axis=1))
    for k in range(CAP):
        of = ids[:, 32 + k:33 + k]
        each = jnp.where(of < 0.5, grads[0], jnp.where(of < 1.5, grads[1], jnp.where(of < 2.5, grads[2], grads[3])))
        high, low = split(each)
        expand[k * lines:(k + 1) * lines, 0:256] = high
        expand[k * lines:(k + 1) * lines, 256:512] = low
    keys = ids.T[0:CAP]

    def sums(offsets):
        for i, d in enumerate(offsets):
            base = c * half_rows + ((y + d + ny) % ny) * nb + 1
            number = (iota((nb, lines), 0) + base).astype(F32)
            for k in range(CAP):
                hits[i * nb:(i + 1) * nb, k * lines:(k + 1) * lines] = one_hot(number == keys[k:k + 1, :])
        both = dot(hits[...], expand[...])
        total = both[:, 0:256] + both[:, 256:512]
        for i, d in enumerate(offsets):
            u[(d + ny) % ny] = total[i * nb:(i + 1) * nb]

    slots = CAP // 3

    def look_up(first):
        if first == 0:
            for copy in x2_copies:
                copy.wait_recv()
        mine = own_lanes(jnp.concatenate([x2buf[j] for j in range(NX)], axis=0))
        for k in range(slots):
            col = mine[:, first + k:first + k + 1]
            number = (iota((ns, rows_dev), 1) + 1).astype(F32)
            look[k * ns:(k + 1) * ns, :] = one_hot(number == col)
        both = dot(look[...], tabs[...])
        found = both[:, 0:256] + both[:, 256:512]
        for b in range(4):
            total = jnp.zeros((ns, 256), F32) if first == 0 else part[b]
            for k in range(slots):
                of = mine[:, 32 + first + k:33 + first + k]
                total = total + jnp.where(of == b, found[k * ns:(k + 1) * ns], 0.0)
            part[b] = total

    def cut(ref, h):
        return ref.at[pl.ds(h * nh, nh)]

    half = ny // 2
    pieces = [(1, 0)] + [(t, h) for t in range(2, half + 1) for h in (1, 0)]
    number_of = {piece: i for i, piece in enumerate(pieces)}
    rs_copies = {}

    def rs_copy(way, t, h):
        i = number_of[(t, h)]
        d = half + 1 - t
        src = cut(u.at[d if way == 0 else (ny - d) % ny], h if way == 0 else 1 - h)
        copy = remote(src, rbuf.at[way, i], rs_send.at[way, i], rs_recv.at[way, i], y_peer[way])
        rs_copies[way, t, h] = copy
        copy.start()

    def rs_take(way, t, h):
        rs_copies[way, t, h].wait_recv()
        i = number_of[(t, h)]
        d = half - t
        hh = h if way == 0 else 1 - h
        slot = d if way == 0 else (ny - d) % ny
        rows = pl.ds(hh * nh, nh)
        u[slot, rows, :] = u[slot, rows, :] + rbuf[way, i]

    px_copies = []

    def pool_x():
        for b in range(4):
            total = part[b]
            for h in range(2):
                psend[pl.ds(b + 4 * h, ns, stride=8), :] = total[:, h * 128:(h + 1) * 128]
        for d in range(1, NX):
            src = psend.at[pl.ds(((x + d) % NX) * gt, gt)]
            px_copies.append(remote(src, pbuf.at[d], px_send.at[d], px_recv.at[d], x_peer(d)))
            px_copies[-1].start()

    rest = [functools.partial(sums, (half + 1 - t, t - half - 1)) for t in range(2, half + 1)]
    rest += [functools.partial(look_up, i * slots) for i in range(3)] + [pool_x]

    def between():
        if rest:
            rest.pop(0)()

    sums((half, 0))
    for way in range(2):
        rs_copy(way, 1, 0)
    between()
    for way in range(2):
        rs_copy(way, 2, 1)
    between()
    for t, h in pieces[:-2]:
        for way in range(2):
            rs_take(way, t, h)
            rs_copy(way, t + 1, h)
        between()
    while rest:
        between()
    for t, h in pieces[-2:]:
        for way in range(2):
            rs_take(way, t, h)

    def block(line, core, h):
        first = core * half_rows + line * nb
        return pl.ds(first, nb) if h is None else pl.ds(first + h * nh, nh)

    def from_line(way, t):
        return (y + ny - t) % ny if way == 0 else (y + t) % ny

    ag_copies, k_copies = {}, {}

    def ag_copy(way, t, h):
        rows = gall.at[block(from_line(way, t - 1), c, h)]
        i = (t - 1) * 2 + h
        ag_copies[way, t, h] = remote(rows, rows, ag_send.at[way, i], ag_recv.at[way, i], y_peer[way])
        ag_copies[way, t, h].start()

    def core_copy(way, t, h):
        rows = gall.at[block(from_line(way, t), c, h)]
        k_copies[way, t] = remote(rows, rows, k_send.at[way, t], k_recv.at[way, t], partner)
        k_copies[way, t].start()

    def update(way, t, h, core):
        line = from_line(way, t)
        rows = block(line, core, h)
        g = gall[rows, :]
        n = g.shape[0]
        at_row = core * ny + line
        eye = iota((n, nb), 0) + (h or 0) * nh == iota((n, nb), 1)
        before = jnp.sum(jnp.where(eye, accbuf[pl.ds(at_row, 1), :], 0.0), axis=1, keepdims=True)
        after = before + jnp.sum(g * g, axis=1, keepdims=True) * (1.0 / g.shape[1])
        new_table[rows, :] = tab[rows, :] - learn_rate * g / jnp.sqrt(after)
        line_after = jnp.sum(jnp.where(eye, after, 0.0), axis=0, keepdims=True)
        if h == 1:
            line_after = line_after + new_accum[pl.ds(at_row, 1), :]
        new_accum[pl.ds(at_row, 1), :] = line_after

    gall[block(y, c, None), :] = u[0]
    for h in range(2):
        for way in range(2):
            ag_copy(way, 1, h if way == 0 else 1 - h)
    core_copy(0, 0, None)

    def pool_z():
        for copy in px_copies:
            copy.wait_recv()
        total = psend[pl.ds(x * gt, gt), :]
        for d in range(1, NX):
            total = total + pbuf[d]
        for i in range(nz):
            qsend[i] = total[i * 8:(i + 1) * 8]
        qbuf[z] = qsend[z]
        lax.fori_loop(0, nz // 2, send_q, 0)

    def pool_z_rest():
        lax.fori_loop(nz // 2, nz - 1, send_q, 0)

    def send_q(i, _):
        d = far_first(i)
        to = (z + d) % nz
        remote(qsend.at[to], qbuf.at[z], pz_sem.at[0], pz_sem.at[1], z_peer(d)).start()
        return 0

    q_all = from_others(qbuf, pz_sem)

    def sent(copies):
        for copy in copies:
            copy.wait_send()

    def update_all(jobs):
        for job in jobs:
            update(*job)

    def update_other(jobs):
        for way, t, h in jobs:
            k_copies[way, t].wait_recv()
            update(way, t, h, 1 - c)

    meanwhile = {
        (1, 0): [lambda: update(0, 0, None, c)],
        (1, 1): [pool_z],
        (2, 0): [pool_z_rest, lambda: sent((z_all, z2_all, *x_copies, *x2_copies, *c_copies))],
    }
    own = lambda t: [(way, t, None, c) for way in range(2)]
    other = lambda t: [(way, t, None) for way in range(2)]
    for t in range(1, half):
        for h in range(2):
            for way in range(2):
                hh = h if way == 0 else 1 - h
                ag_copies[way, t, hh].wait_recv()
                if t + 1 < half or hh == way:
                    ag_copy(way, t + 1, hh)
                if h == 1:
                    core_copy(way, t, None)
            for job in meanwhile.pop((t, h), []):
                job()
            if h == 0 and t > 1:
                update_all(own(t - 1))
            if h == 1:
                update_other(other(t - 1) if t > 1 else [(0, 0, None)])
    for jobs in meanwhile.values():
        for job in jobs:
            job()
    update_all(own(half - 1))
    sent((*px_copies, *rs_copies.values()))
    for way in range(2):
        ag_copies[way, half, way].wait_recv()
        core_copy(way, half, way)
    update_other(other(half - 1))
    for way in range(2):
        update(way, half, way, c)
    q_all.wait_recv()
    total = qbuf[0]
    for i in range(1, nz):
        total = total + qbuf[i]
    pooled[:, 0:128] = total[0:4]
    pooled[:, 128:256] = total[4:8]
    sent((q_all, *ag_copies.values()))
    for way in range(2):
        k_copies[way, half].wait_recv()
        update(way, half, way, 1 - c)
    sent(k_copies.values())


def hand_on(pooled, new_table, new_accum, pooled_out, table_out, accum_out, sems):
    copies = [
        pltpu.make_async_copy(src, dst, sems.at[i])
        for i, (src, dst) in enumerate(
            ((new_table, table_out), (pooled, pooled_out), (new_accum, accum_out))
        )
    ]
    for copy in copies:
        copy.start()
    for copy in copies:
        copy.wait()


def local(
    ny, nz,
    item_table, row_accum, owner_map, row_index, bag_index, prev_owner, prev_row, prev_bag, grad_pooled,
):
    rows_dev, width = item_table.shape
    bags = grad_pooled.shape[2]
    n = row_index.shape[2]
    half_rows = rows_dev // 2
    nb = half_rows // ny
    nh = nb // 2
    ns, gt, half = NX * nz, nz * 8, ny // 2
    lines = 2 * ns
    line = lambda a: a.reshape(1, n)
    vmem = pl.BlockSpec(memory_space=pltpu.VMEM)
    hbm = pl.BlockSpec(memory_space=pl.ANY)
    dma = pltpu.SemaphoreType.DMA
    sums = [
        ((bags, width), F32),
        ((rows_dev, width), F32),
        ((rows_dev // nb, nb), F32),
    ]
    inputs = (
        *(line(v) for v in (owner_map, row_index, bag_index, prev_owner, prev_row, prev_bag)),
        grad_pooled.reshape(bags, width), row_accum.reshape(rows_dev // nb, nb), item_table,
    )
    results = pl.pallas_call(
        functools.partial(kernel, ny, nz),
        out_shape=[jax.ShapeDtypeStruct(*s) for s in sums],
        in_specs=[pl.BlockSpec(memory_space=pltpu.HBM)] * 9,
        out_specs=[vmem] * 3,
        scratch_shapes=[
            pltpu.VMEM((6, 1, n), I32),
            pltpu.VMEM((bags, width), F32),
            pltpu.VMEM((rows_dev // nb, nb), F32),
            dma((8,)),
            pltpu.VMEM((rows_dev, width), F32),
            pltpu.VMEM((rows_dev, 2 * width), BF16),
            pltpu.VMEM((nz, 10, 128), F32),
            pltpu.VMEM((nz, 10, 128), F32),
            pltpu.VMEM((nz, 2, 128), F32),
            pltpu.VMEM((nz, 2, 128), F32),
            pltpu.VMEM((NX, gt + nz, 128), F32),
            pltpu.VMEM((2, NX, gt + nz, 128), F32),
            pltpu.VMEM((NX, nz, 128), F32),
            pltpu.VMEM((NX, nz, 128), F32),
            pltpu.VMEM((CAP * lines, 2 * width), BF16),
            pltpu.VMEM((2 * nb, CAP * lines), BF16),
            pltpu.VMEM((CAP // 3 * ns, rows_dev), BF16),
            pltpu.VMEM((4, ns, width), F32),
            pltpu.VMEM((ns * 8, 128), F32),
            pltpu.VMEM((NX, gt, 128), F32),
            pltpu.VMEM((nz, 8, 128), F32),
            pltpu.VMEM((nz, 8, 128), F32),
            pltpu.VMEM((ny, nb, width), F32),
            pltpu.VMEM((2, 2 * half - 1, nh, width), F32),
            pltpu.VMEM((rows_dev, width), F32),
            dma(()), dma((2,)), dma((2,)),
            dma((NX,)), dma((NX,)), dma((NX,)), dma((NX,)), dma((NX,)), dma((NX,)),
            dma((2, 2 * half)), dma((2, 2 * half)),
            dma((2, 2 * half)), dma((2, 2 * half)),
            dma((2, half + 1)), dma((2, half + 1)),
            dma((NX,)), dma((NX,)), dma((2,)),
        ],
        compiler_params=pltpu.CompilerParams(
            collective_id=0, has_side_effects=True, vmem_limit_bytes=40 * 1024 * 1024
        ),
    )(
        *(pltpu.with_memory_space_constraint(v, pltpu.HBM) for v in inputs)
    )
    pooled, new_table, new_accum = pl.pallas_call(
        hand_on,
        out_shape=[jax.ShapeDtypeStruct(*s) for s in sums],
        in_specs=[vmem] * 3,
        out_specs=[hbm] * 3,
        scratch_shapes=[dma((3,))],
        compiler_params=pltpu.CompilerParams(vmem_limit_bytes=4 * 1024 * 1024),
    )(*results)
    return (
        pooled.reshape(1, 1, bags, width),
        new_table,
        new_accum.reshape(rows_dev),
    )


def solution(mesh):
    ny, nz = mesh.shape["dp"] // 2, mesh.shape["rows"] // NX
    placed = (
        P("rows", None),
        P("rows"),
        P("dp", "rows", None, None),
        P("dp", "rows", None),
        P("dp", "rows", None),
        P("dp", "rows", None, None),
        P("dp", "rows", None),
        P("dp", "rows", None),
        P("dp", "rows", None, None),
    )
    return jax.shard_map(
        functools.partial(local, ny, nz),
        mesh=mesh,
        in_specs=placed,
        out_specs=(P("dp", "rows", None, None), P("rows", None), P("rows")),
        check_vma=False,
    )
```

time: 85 us -> 76.8 us (0.904)
  local copies, waits for them, and re-layouts: 4.93 us -> 0 us
  Pallas kernels: 78.6 us -> 75.9 us
    unnamed x5 -> x0, local copies, waits for them, and re-layouts: 4.93 us -> none
    pallas_call x1, Pallas kernels: 78.6 us -> 74.5 us  [local(): pl.pallas_call(functools.partial(kernel, ny, nz), out_shape=[jax.ShapeDty...]
    pallas_call x0 -> x1, Pallas kernels: none -> 1.35 us  [local(): pl.pallas_call(hand_on, out_shape=[jax.ShapeDtypeStruct(*s) for s in sums...]
where the time goes in v2:
time: 76.8 us; the launch traced here: 76.5 us
  Pallas kernels  75.9 us (99%)
    pallas_call x1, Pallas kernels, local(): pl.pallas_call(functools.partial(kernel, ny, nz), out_shape=[jax.ShapeDty...  74.5 us

profile of v2, /device:TPU:1, one launch (start us, length us, event | category | flops | bytes accessed | tf_op | source)
XLA Modules:
  0.0 76.5 jit_solution(16674069114864091758)
XLA Ops:
  0.6 74.5 %shard_map.112 = (f32[4,256]{1,0:T(4,128)S(1)}, f32[2048,256]{1,0:T(8,128)S(1)}, f32[16,128]{1,0:T(8,128)S(1)}) custom-call(s32[1,512]{1,0:T(1,128)} %bitcast.12, s32[1,512]{1,0:T(1,128)} %bitcast.13, s32[1,512]{1,0:T(1,128)} %bitcast.14, s32[1,512]{1,0:T(1,128)} %bitcast.15, s32[1,512]{1,0:T(1,128)} %bitcast.16, s32[1,512]{1,0:T(1,128)} %bitcast.17, ...), custom_call_target="tpu_custom_call" | custom-call | tf_op jit(solution)/shard_map/pallas_call | solution.py:490
  75.2 1.4 %shard_map.113 = (f32[4,256]{1,0:T(4,128)}, f32[2048,256]{1,0:T(8,128)}, f32[16,128]{1,0:T(8,128)}) custom-call(f32[4,256]{1,0:T(4,128)S(1)} %get-tuple-element.9.pooled, f32[2048,256]{1,0:T(8,128)S(1)} %get-tuple-element.10.new_table, f32[16,128]{1,0:T(8,128)S(1)} %get-tuple-element.11.new_accum), custom_call_target="tpu_custom_call" | custom-call | tf_op jit(solution)/shard_map/pallas_call | solution.py:534

commit v3 on v2

--- a/solution.py
+++ b/solution.py
@@ -72,9 +72,9 @@
     ny, nz,
     owner, row, bag, powner, prow, pbag, grad, accum, table,
     pooled, new_table, new_accum,
-    idbuf, gradbuf, accbuf, in_sem, tab, tabs, zsend, zbuf, z2send, z2buf, xsend, xbuf, x2send, x2buf,
+    idbuf, gradbuf, accbuf, in_sem, tab, tabs, zsend, zbuf, xsend, xbuf, x2send, x2buf,
     expand, hits, look, part, psend, pbuf, qsend, qbuf, u, rbuf, gall,
-    tab_sem, z_sem, z2_sem, x_send, x_recv, x2_send, x2_recv, c_send, c_recv,
+    tab_sem, z_sem, x_send, x_recv, x2_send, x2_recv, c_send, c_recv,
     rs_send, rs_recv, ag_send, ag_recv, k_send, k_recv, px_send, px_recv, pz_sem,
 ):
     dp, rw = lax.axis_index("dp"), lax.axis_index("rows")
@@ -140,8 +140,7 @@
     tile = jnp.concatenate([g4[:, :128], g4[:, 128:]], axis=0)
     for i in range(nz):
         zsend[i, 0:8, :] = tile
-        zsend[i, 8:10, :] = message[i * 8:i * 8 + 2]
-        z2send[i] = message[i * 8 + 2:i * 8 + 4]
+        zsend[i, 8:12, :] = message[i * 8:i * 8 + 4]
     pl.semaphore_wait(barrier, nz - 1 + NX - 1 + 1 + 2)
 
     def send_z(i, _):
@@ -150,29 +149,35 @@
         remote(zsend.at[to], zbuf.at[z], z_sem.at[0], z_sem.at[1], z_peer(d)).start()
         return 0
 
-    def send_z2(i, _):
-        d = far_first(i)
-        to = (z + d) % nz
-        remote(z2send.at[to], z2buf.at[z], z2_sem.at[0], z2_sem.at[1], z_peer(d)).start()
-        return 0
-
     def from_others(buf, sems):
         others = buf.at[pl.ds(0, nz - 1)]
         return remote(others, others, sems.at[0], sems.at[1], z_peer(1))
 
     lax.fori_loop(0, nz - 1, send_z, 0)
-    lax.fori_loop(0, nz - 1, send_z2, 0)
     zbuf[z] = zsend[z]
-    z2buf[z] = z2send[z]
-    z_all, z2_all = from_others(zbuf, z_sem), from_others(z2buf, z2_sem)
+    z_all = from_others(zbuf, z_sem)
+
+    for copy in loads:
+        copy.wait()
+    high, low = split(tab[...])
+    tabs[:, 0:256] = high
+    tabs[:, 256:512] = low
     z_all.wait_recv()
 
+    for i in range(NX):
+        x2send[i] = zbuf[:, 10 + i // 2, :]
+    x2_copies = []
+    for d in range(1, NX):
+        x2_copies.append(
+            remote(x2send.at[(x + d) % NX], x2buf.at[x], x2_send.at[d], x2_recv.at[d], x_peer(d))
+        )
+        x2_copies[-1].start()
     for i in range(NX):
         for j in range(nz):
             xsend[i, j * 8:(j + 1) * 8, :] = zbuf[j, 0:8, :]
         xsend[i, gt:gt + nz, :] = zbuf[:, 8 + i // 2, :]
     x_copies = []
-    for d in range(1, NX):
+    for d in (2, 1, 3):
         x_copies.append(
             remote(xsend.at[(x + d) % NX], xbuf.at[c, x], x_send.at[d], x_recv.at[d], x_peer(d))
         )
@@ -181,69 +186,10 @@
     own = xbuf.at[c, x]
     c_copies = [remote(own, own, c_send.at[0], c_recv.at[0], partner)]
     c_copies[0].start()
-    z2_all.wait_recv()
-    for i in range(NX):
-        x2send[i] = z2buf[:, i // 2, :]
-    x2_copies = []
-    for d in range(1, NX):
-        x2_copies.append(
-            remote(x2send.at[(x + d) % NX], x2buf.at[x], x2_send.at[d], x2_recv.at[d], x_peer(d))
-        )
-        x2_copies[-1].start()
     x2buf[x] = x2send[x]
-    for d in range(1, NX):
-        x_copies[d - 1].wait_recv()
-        piece = xbuf.at[c, (x + NX - d) % NX]
-        c_copies.append(remote(piece, piece, c_send.at[d], c_recv.at[d], partner))
-        c_copies[-1].start()
-
-    for copy in loads:
-        copy.wait()
-    high, low = split(tab[...])
-    tabs[:, 0:256] = high
-    tabs[:, 256:512] = low
-    for copy in c_copies:
-        copy.wait_recv()
 
     def own_lanes(v):
         return jnp.where(x % 2 == 0, v, pltpu.roll(v, 64, 1))
-
-    ids = own_lanes(
-        jnp.concatenate([xbuf[i, j, gt:gt + nz, :] for i in range(2) for j in range(NX)], axis=0)
-    )
-    lines = 2 * ns
-    grads = []
-    for b in range(4):
-        sides = [
-            jnp.concatenate(
-                [
-                    xbuf[i, j, pl.ds(b + 4 * h, nz, stride=8), :]
-                    for i in range(2)
-                    for j in range(NX)
-                ],
-                axis=0,
-            )
-            for h in range(2)
-        ]
-        grads.append(jnp.concatenate(sides, axis=1))
-    for k in range(CAP):
-        of = ids[:, 32 + k:33 + k]
-        each = jnp.where(of < 0.5, grads[0], jnp.where(of < 1.5, grads[1], jnp.where(of < 2.5, grads[2], grads[3])))
-        high, low = split(each)
-        expand[k * lines:(k + 1) * lines, 0:256] = high
-        expand[k * lines:(k + 1) * lines, 256:512] = low
-    keys = ids.T[0:CAP]
-
-    def sums(offsets):
-        for i, d in enumerate(offsets):
-            base = c * half_rows + ((y + d + ny) % ny) * nb + 1
-            number = (iota((nb, lines), 0) + base).astype(F32)
-            for k in range(CAP):
-                hits[i * nb:(i + 1) * nb, k * lines:(k + 1) * lines] = one_hot(number == keys[k:k + 1, :])
-        both = dot(hits[...], expand[...])
-        total = both[:, 0:256] + both[:, 256:512]
-        for i, d in enumerate(offsets):
-            u[(d + ny) % ny] = total[i * nb:(i + 1) * nb]
 
     slots = CAP // 3
 
@@ -265,6 +211,54 @@
                 total = total + jnp.where(of == b, found[k * ns:(k + 1) * ns], 0.0)
             part[b] = total
 
+    look_up(0)
+
+    lines = 2 * ns
+
+    def expand_piece(i, j):
+        ids = own_lanes(xbuf[i, j, gt:gt + nz, :])
+        grads = [
+            jnp.concatenate(
+                [xbuf[i, j, pl.ds(b + 4 * h, nz, stride=8), :] for h in range(2)], axis=1
+            )
+            for b in range(4)
+        ]
+        for k in range(CAP):
+            of = ids[:, 32 + k:33 + k]
+            low_half = jnp.where(of < 0.5, grads[0], grads[1])
+            high, low = split(jnp.where(of < 1.5, low_half, jnp.where(of < 2.5, grads[2], grads[3])))
+            expand[k, i * NX + j, :, 0:256] = high
+            expand[k, i * NX + j, :, 256:512] = low
+
+    expand_piece(c, x)
+    for n, d in enumerate((1, 3, 2)):
+        x_copies[(2, 1, 3).index(d)].wait_recv()
+        piece = xbuf.at[c, (x + NX - d) % NX]
+        c_copies.append(remote(piece, piece, c_send.at[d], c_recv.at[d], partner))
+        c_copies[-1].start()
+        if n > 0:
+            expand_piece(c, (x + NX - (1, 3, 2)[n - 1]) % NX)
+    expand_piece(c, (x + NX - 2) % NX)
+    for copy, d in zip(c_copies, (0, 1, 3, 2)):
+        copy.wait_recv()
+        expand_piece(1 - c, (x + NX - d) % NX)
+    ids = own_lanes(
+        jnp.concatenate([xbuf[i, j, gt:gt + nz, :] for i in range(2) for j in range(NX)], axis=0)
+    )
+    keys = ids.T[0:CAP]
+
+    def sums(offsets):
+        for i, d in enumerate(offsets):
+            base = c * half_rows + ((y + d + ny) % ny) * nb + 1
+            number = (iota((nb, lines), 0) + base).astype(F32)
+            for k in range(CAP):
+                hits[i * nb:(i + 1) * nb, k * lines:(k + 1) * lines] = one_hot(number == keys[k:k + 1, :])
+        many = len(offsets) * nb
+        both = dot(hits[0:many], expand[...].reshape(CAP * lines, expand.shape[-1]))
+        total = both[:, 0:256] + both[:, 256:512]
+        for i, d in enumerate(offsets):
+            u[(d + ny) % ny] = total[i * nb:(i + 1) * nb]
+
     def cut(ref, h):
         return ref.at[pl.ds(h * nh, nh)]
 
@@ -303,13 +297,13 @@
             px_copies[-1].start()
 
     rest = [functools.partial(sums, (half + 1 - t, t - half - 1)) for t in range(2, half + 1)]
-    rest += [functools.partial(look_up, i * slots) for i in range(3)] + [pool_x]
+    rest += [functools.partial(look_up, i * slots) for i in (1, 2)] + [lambda: (pool_x(), sums((0,)))]
 
     def between():
         if rest:
             rest.pop(0)()
 
-    sums((half, 0))
+    sums((half,))
     for way in range(2):
         rs_copy(way, 1, 0)
     between()
@@ -406,7 +400,7 @@
     meanwhile = {
         (1, 0): [lambda: update(0, 0, None, c)],
         (1, 1): [pool_z],
-        (2, 0): [pool_z_rest, lambda: sent((z_all, z2_all, *x_copies, *x2_copies, *c_copies))],
+        (2, 0): [pool_z_rest, lambda: sent((z_all, *x_copies, *x2_copies, *c_copies))],
     }
     own = lambda t: [(way, t, None, c) for way in range(2)]
     other = lambda t: [(way, t, None) for way in range(2)]
@@ -499,15 +493,13 @@
             dma((8,)),
             pltpu.VMEM((rows_dev, width), F32),
             pltpu.VMEM((rows_dev, 2 * width), BF16),
-            pltpu.VMEM((nz, 10, 128), F32),
-            pltpu.VMEM((nz, 10, 128), F32),
-            pltpu.VMEM((nz, 2, 128), F32),
-            pltpu.VMEM((nz, 2, 128), F32),
+            pltpu.VMEM((nz, 12, 128), F32),
+            pltpu.VMEM((nz, 12, 128), F32),
             pltpu.VMEM((NX, gt + nz, 128), F32),
             pltpu.VMEM((2, NX, gt + nz, 128), F32),
             pltpu.VMEM((NX, nz, 128), F32),
             pltpu.VMEM((NX, nz, 128), F32),
-            pltpu.VMEM((CAP * lines, 2 * width), BF16),
+            pltpu.VMEM((CAP, 2 * NX, nz, 2 * width), BF16),
             pltpu.VMEM((2 * nb, CAP * lines), BF16),
             pltpu.VMEM((CAP // 3 * ns, rows_dev), BF16),
             pltpu.VMEM((4, ns, width), F32),
@@ -518,7 +510,7 @@
             pltpu.VMEM((ny, nb, width), F32),
             pltpu.VMEM((2, 2 * half - 1, nh, width), F32),
             pltpu.VMEM((rows_dev, width), F32),
-            dma(()), dma((2,)), dma((2,)),
+            dma(()), dma((2,)),
             dma((NX,)), dma((NX,)), dma((NX,)), dma((NX,)), dma((NX,)), dma((NX,)),
             dma((2, 2 * half)), dma((2, 2 * half)),
             dma((2, 2 * half)), dma((2, 2 * half)),

time: 76.8 us -> 76.8 us (level)
  no operation moved by 1% of the time
where the time goes in v3:
time: 76.8 us; the launch traced here: 76.3 us
  Pallas kernels  75.7 us (99%)
    pallas_call x1, Pallas kernels, local(): pl.pallas_call(functools.partial(kernel, ny, nz), out_shape=[jax.ShapeDty...  74.3 us

profile of v3, /device:TPU:1, one launch (start us, length us, event | category | flops | bytes accessed | tf_op | source)
XLA Modules:
  0.0 76.3 jit_solution(6258637615030676067)
XLA Ops:
  0.6 74.3 %shard_map.112 = (f32[4,256]{1,0:T(4,128)S(1)}, f32[2048,256]{1,0:T(8,128)S(1)}, f32[16,128]{1,0:T(8,128)S(1)}) custom-call(s32[1,512]{1,0:T(1,128)} %bitcast.12, s32[1,512]{1,0:T(1,128)} %bitcast.13, s32[1,512]{1,0:T(1,128)} %bitcast.14, s32[1,512]{1,0:T(1,128)} %bitcast.15, s32[1,512]{1,0:T(1,128)} %bitcast.16, s32[1,512]{1,0:T(1,128)} %bitcast.17, ...), custom_call_target="tpu_custom_call" | custom-call | tf_op jit(solution)/shard_map/pallas_call | solution.py:484
  75.0 1.4 %shard_map.113 = (f32[4,256]{1,0:T(4,128)}, f32[2048,256]{1,0:T(8,128)}, f32[16,128]{1,0:T(8,128)}) custom-call(f32[4,256]{1,0:T(4,128)S(1)} %get-tuple-element.9.pooled, f32[2048,256]{1,0:T(8,128)S(1)} %get-tuple-element.10.new_table, f32[16,128]{1,0:T(8,128)S(1)} %get-tuple-element.11.new_accum), custom_call_target="tpu_custom_call" | custom-call | tf_op jit(solution)/shard_map/pallas_call | solution.py:526
